TPU v7x, 128 devices: a whole 4x4x4 slice. The times are simulated.
128 devices in a mesh: seq: 16 (over y, x_lo, core), tensor: 8 (over z, x_hi).
Axes of the slice: x: 4 (x_hi: 2, x_lo: 2; x = x_hi * 2 + x_lo), y: 4, z: 4, core: 2. Of those that a mesh axis runs over, the one named last changes fastest.
Arguments:
- tokens: bfloat16 [2048, 16384], P('seq', 'tensor'), may hold values from -100 to 100
- norm_gain: float32 [16384], P('tensor'), may hold values from 0.5 to 1.5
- projection_weight: bfloat16 [2048, 16384], P('tensor', 'seq'), may hold values from -1.5 to 1.5
- panel_index: int32 [1], replicated, may hold values from 0 to 31
Outputs:
- gram: float32 [16384, 16384], P('seq', 'tensor')
- factor_panel: bfloat16 [16384, 512], P('seq')
- projected: float32 [2048, 512], P('tensor', 'seq')
All inputs are finite; a program needn't handle non-finite values.
Results may differ from a plain program's by a relative error of at most 0.0057.
Values may be sent and summed in bfloat16 or wider, within the bound.
A program may use at most 128 MiB of HBM per device.

v0:
```python
import jax
import jax.numpy as jnp
from jax import lax
from jax.sharding import PartitionSpec as P

D = 16384
PANEL = 512
epsilon = 1e-05
damping = 0.1


def broadcast(value, axis, source):
    kept = jnp.where(lax.axis_index(axis) == source, value, 0).astype(value.dtype)
    return lax.psum(kept, axis)


def on_device(tokens, norm_gain, projection_weight, panel_index):
    token_values = tokens.astype(jnp.float32)
    squares = lax.psum(jnp.sum(token_values * token_values, axis=1), "tensor")
    scaled = token_values * lax.rsqrt(squares / D + epsilon)[:, None] * norm_gain[None, :]
    normed = scaled.astype(jnp.bfloat16)
    column_width = normed.shape[1]
    row_width = column_width * lax.axis_size("tensor") // lax.axis_size("seq")
    blocks = column_width // row_width
    seq_index = lax.axis_index("seq")
    tensor_index = lax.axis_index("tensor")
    columns = lax.all_gather(normed, "seq", axis=0, tiled=True)
    local_rows = lax.dynamic_slice_in_dim(columns, seq_index % blocks * row_width, row_width, 1)
    row_part = broadcast(local_rows, "tensor", seq_index // blocks)
    tokens_all = columns.shape[0]
    gram_tile = (
        lax.dot_general(
            row_part, columns, (((0,), (0,)), ((), ())), preferred_element_type=jnp.float32
        )
        / tokens_all
    )
    normed_wide = normed.astype(jnp.float32)
    trace_sum = lax.psum(jnp.sum(normed_wide * normed_wide), ("seq", "tensor")) / tokens_all
    diag_shift = damping * trace_sum / D
    row_ids = seq_index * row_width + lax.iota(jnp.int32, row_width)
    col_ids = tensor_index * column_width + lax.iota(jnp.int32, column_width)
    shifted = gram_tile + jnp.where(
        row_ids[:, None] == col_ids[None, :], diag_shift, jnp.float32(0.0)
    )
    panel_start = panel_index[0] * PANEL
    owner_column = panel_start // column_width
    offset = panel_start - owner_column * column_width
    panel_rows = lax.dynamic_slice_in_dim(shifted, offset, PANEL, 1)
    piece_rows = min(PANEL, row_width)
    global_row = panel_start + 0
    source = global_row // row_width
    local_offset = global_row - source * row_width
    piece = lax.dynamic_slice_in_dim(panel_rows, local_offset, piece_rows, 0)
    pieces = broadcast(piece, "seq", source)
    diag_block = pieces
    identity = jnp.eye(PANEL, dtype=jnp.float32)
    diag_block = jnp.where(tensor_index == owner_column, diag_block, identity)
    factor = jnp.linalg.cholesky(diag_block)
    solved = lax.linalg.triangular_solve(
        factor, panel_rows, left_side=False, lower=True, transpose_a=True
    )
    whitened_rows = solved.astype(jnp.bfloat16)
    whitened_full = broadcast(whitened_rows, "tensor", owner_column)
    partial_value = jnp.dot(projection_weight, whitened_full, preferred_element_type=jnp.float32)
    projected = lax.psum_scatter(partial_value, "seq", scatter_dimension=1, tiled=True)
    return (shifted, whitened_full, projected)


def solution(mesh):
    placed = (P("seq", "tensor"), P("tensor"), P("tensor", "seq"), P())
    return jax.shard_map(
        on_device,
        mesh=mesh,
        in_specs=placed,
        out_specs=(P("seq", "tensor"), P("seq", None), P("tensor", "seq")),
        check_vma=False,
    )
```

profile of v0, /device:TPU:0, one launch (start us, length us, event | category | flops | bytes accessed | tf_op | source)
XLA Modules:
  0.0 742.1 jit_solution(978973545675533625)
XLA Ops:
  7.2 1.3 fusion.9
  8.5 25.6 %psum.35 = f32[128]{0:T(128)S(1)} all-reduce(f32[128]{0:T(128)S(1)} %fusion.9), channel_id=1, replica_groups=mesh['seq'=16,'tensor'=8] {'tensor'}, use_global_device_ids=true, to_apply=%region_1.0 | all-reduce | flops 128 | bytes 1024 | tf_op jit(solution)/shard_map/psum | solution.py:19
  34.1 2.7 multiply_reduce_fusion
  36.9 48.6 %all-gather.2.cloned.1.call-done = bf16[2048,2048]{1,0:T(8,128)(2,1)} async-done(((bf16[128,2048]{1,0:T(8,128)(2,1)}), bf16[2048,2048]{1,0:T(8,128)(2,1)}) %all-gather.2.cloned.1.call-update) | async-done | bytes 8388624 | tf_op jit(solution)/shard_map/all_gather | solution.py:27
  85.5 5.4 dynamic-slice_select_fusion
  91.0 209.9 %psum.37 = f32[]{:T(128)} all-reduce(f32[]{:T(128)} %get-tuple-element.26), channel_id=1, replica_groups=mesh['seq'=16,'tensor'=8] {'seq','tensor'}, use_global_device_ids=true, to_apply=%region_4.5 | all-reduce | flops 1 | bytes 8 | tf_op jit(solution)/shard_map/psum | solution.py:38
  302.3 13.0 %select_add_fusion = f32[1024,2048]{0,1:T(8,128)S(1)} fusion(bf16[2048,1024]{1,0:T(8,128)(2,1)} %all-reduce.5.cloned.1.call-done, bf16[2048,2048]{1,0:T(8,128)(2,1)} %all-gather.2.cloned.1.call-done, f32[]{:T(128)S(6)} %div.53, s32[1024]{0:T(1024)S(1)} %iota_add_fusion.1, s32[2048]{0:T(1024)S(1)} %iota_add_fusion), kind=kOutput, calls=%fused_computation.2 | convolution fusion | flops 8598323200 | bytes 20983812 | tf_op jit(solution)/shard_map/dot_general | solution.py:32
  315.4 3.2 copy-done.1
  318.6 1.3 dynamic-slice_select_fusion.1
  319.9 0.5 all-reduce.9.cloned.1.call-start
  320.5 116.3 %all-reduce.7.cloned.1.call-done = f32[512,512]{0,1:T(8,128)} async-done(((f32[512,512]{0,1:T(8,128)}), f32[512,512]{0,1:T(8,128)}) %all-reduce.7.cloned.1.call-update) | async-done | bytes 1048592 | tf_op jit(solution)/shard_map/psum | solution.py:14
  436.8 0.1 convert_select_fusion
  436.9 1.3 copy.8
  438.2 1.5 fusion.15
  439.7 11.7 %cholesky.103 = f32[128,128]{1,0:T(8,128)S(1)} custom-call(f32[128,128]{1,0:T(8,128)S(1)} %cholesky.263), custom_call_target="Cholesky" | custom-call | tf_op jit(solution)/shard_map/jit(cholesky)/cholesky | solution.py:58
  451.4 9.8 %custom-call.30 = f32[1,128,128]{1,2,0:T(8,128)S(1)} custom-call(f32[1,128,128]{2,1,0:T(8,128)S(1)} %get-tuple-element.35), custom_call_target="InvertDiagBlocksLowerTriangular" | custom-call | tf_op jit(solution)/shard_map/jit(cholesky)/cholesky | solution.py:58
  461.2 0.3 fusion.21
  461.6 0.3 convolution_subtract_fusion.2
  461.9 11.7 %cholesky.215 = f32[128,128]{1,0:T(8,128)S(1)} custom-call(f32[128,128]{1,0:T(8,128)S(1)} %cholesky.267), custom_call_target="Cholesky" | custom-call | tf_op jit(solution)/shard_map/jit(cholesky)/cholesky | solution.py:58
  473.7 0.1 copy.11
  473.8 0.1 copy.10
  473.9 0.1 copy.9
  474.0 9.9 %custom-call.31 = f32[1,128,128]{1,2,0:T(8,128)S(1)} custom-call(f32[1,128,128]{2,1,0:T(8,128)S(1)} %get-tuple-element.33), custom_call_target="InvertDiagBlocksLowerTriangular" | custom-call | tf_op jit(solution)/shard_map/jit(cholesky)/cholesky | solution.py:58
  483.9 0.1 cholesky.222
  484.1 0.3 convolution_dynamic-update-slice_fusion
  484.4 0.6 convolution_subtract_fusion.3
  485.0 11.7 %cholesky.236 = f32[128,128]{1,0:T(8,128)S(1)} custom-call(f32[128,128]{1,0:T(8,128)S(1)} %cholesky.272), custom_call_target="Cholesky" | custom-call | tf_op jit(solution)/shard_map/jit(cholesky)/cholesky | solution.py:58
  496.8 0.1 copy.13
  496.9 9.8 %custom-call.32 = f32[1,128,128]{1,2,0:T(8,128)S(1)} custom-call(f32[1,128,128]{2,1,0:T(8,128)S(1)} %get-tuple-element.31), custom_call_target="InvertDiagBlocksLowerTriangular" | custom-call | tf_op jit(solution)/shard_map/jit(cholesky)/cholesky | solution.py:58
  506.7 0.3 convolution_dynamic-update-slice_fusion.1
  507.0 0.5 convolution_subtract_fusion.4
  507.5 11.9 %cholesky.253 = f32[128,128]{1,0:T(8,128)S(1)} custom-call(f32[128,128]{1,0:T(8,128)S(1)} %convolution_subtract_fusion.4), custom_call_target="Cholesky" | custom-call | tf_op jit(solution)/shard_map/jit(cholesky)/cholesky | solution.py:58
  519.4 0.1 copy.15
  519.5 0.6 compare_reduce_fusion.1
  520.2 0.6 compare_reduce_fusion
  520.8 0.6 compare_reduce_fusion.2
  524.0 0.1 select_select_fusion
  524.1 8.5 %while.1 = (s32[]{:T(128)}, f32[512,512]{0,1:T(8,128)S(1)}, s32[4,2]{0,1:T(2,128)S(1)}, f32[4,128,128]{2,1,0:T(8,128)S(1)}, s32[]{:T(128)}) while((s32[]{:T(128)}, f32[512,512]{0,1:T(8,128)S(1)}, s32[4,2]{0,1:T(2,128)S(1)}, f32[4,128,128]{2,1,0:T(8,128)S(1)}, s32[]{:T(128)}) %tuple.33), condition=%wide.while_cond, body=%wide.while_body.sunk | while | flops 2 | bytes 393321 | solution.py:59
  524.2 0.5 fusion.52
  524.7 1.4 dynamic-slice.18
  526.1 0.1 copy.24
  526.3 0.5 fusion.52
  526.8 1.4 dynamic-slice.18
  528.2 0.1 copy.24
  528.4 0.5 fusion.52
  528.9 1.4 dynamic-slice.18
  530.3 0.1 copy.24
  530.5 0.5 fusion.52
  531.1 1.4 dynamic-slice.18
  532.4 0.1 copy.24
  532.6 39.3 %custom-call.33 = f32[4,128,128]{1,2,0:T(8,128)S(1)} custom-call(f32[4,128,128]{2,1,0:T(8,128)S(1)} %get-tuple-element.10), custom_call_target="InvertDiagBlocksLowerTriangular" | custom-call | tf_op jit(solution)/shard_map/triangular_solve | solution.py:59
  571.9 1.7 fusion.41
  573.6 1.7 convolution_subtract_fusion.1
  575.2 0.6 fusion.40
  575.8 1.8 convolution_subtract_fusion
  577.6 0.6 fusion.39
  578.3 2.2 fusion.6
  580.5 0.6 convolution_convert_fusion
  581.1 1.2 maximum_select_fusion
  582.4 91.5 %all-reduce.9.cloned.1.call-done = bf16[1024,512]{0,1:T(8,128)(2,1)} async-done(((bf16[1024,512]{0,1:T(8,128)(2,1)}), bf16[1024,512]{0,1:T(8,128)(2,1)}) %all-reduce.9.cloned.1.call-update) | async-done | bytes 1048592 | tf_op jit(solution)/shard_map/psum | solution.py:14
  673.9 2.5 convolution_bitcast_fusion
  676.5 9.2 %copy.17 = f32[1024,2048]{1,0:T(8,128)} copy(f32[1024,2048]{0,1:T(8,128)} %copy-done.1) | data formatting | bytes 16777216
  685.7 1.3 copy.18
  687.0 48.4 %reduce-scatter.2.cloned.1.call-done = f32[256,32]{0,1:T(8,128)} async-done(((f32[256,512]{0,1:T(8,128)}), f32[256,32]{0,1:T(8,128)}) %reduce-scatter.2.cloned.1.call-update) | async-done | bytes 32784 | tf_op jit(solution)/shard_map/reduce_scatter | solution.py:65
  (42 shorter events, 0.9 us)
Async XLA Ops:
  7.2 666.8 %copy-start = (bf16[256,1024]{1,0:T(8,128)(2,1)S(1)}, bf16[256,1024]{1,0:T(8,128)(2,1)}, u32[]{:S(2)}) copy-start(bf16[256,1024]{1,0:T(8,128)(2,1)} %param.6) | copy-start | bytes 1572868
  7.2 78.4 %all-gather.2.cloned.1.call-start = ((), (), s32[]{:S(2)}) async-start(), calls=%async_computation.1 | async-start | bytes 8912896 | tf_op jit(solution)/shard_map/all_gather | solution.py:27
  36.8 265.5 %all-reduce.5.cloned.1.call-start = ((), (), s32[]{:S(2)}) async-start(), calls=%async_computation.2 | async-start | bytes 8388608 | tf_op jit(solution)/shard_map/psum | solution.py:14
  91.0 345.8 %all-reduce.7.cloned.1.call-start = ((), (), s32[]{:S(2)}) async-start(), calls=%async_computation.3 | async-start | bytes 2097152 | tf_op jit(solution)/shard_map/psum | solution.py:14
  315.4 3.2 copy-start.1
  319.9 354.0 %all-reduce.9.cloned.1.call-start = ((), (), s32[]{:S(2)}) async-start(), calls=%async_computation.4 | async-start | bytes 2097152 | tf_op jit(solution)/shard_map/psum | solution.py:14
  436.8 1.4 copy-start.2
  582.3 153.0 %reduce-scatter.2.cloned.1.call-start = ((), (), s32[]{:S(2)}) async-start(), calls=%async_computation.5 | async-start | bytes 557056 | tf_op jit(solution)/shard_map/reduce_scatter | solution.py:65
  676.5 9.2 %copy-start.3 = (bf16[1024,512]{0,1:T(8,128)(2,1)S(1)}, bf16[1024,512]{0,1:T(8,128)(2,1)}, u32[]{:S(2)}) copy-start(bf16[1024,512]{0,1:T(8,128)(2,1)} %all-reduce.9.cloned.1.call-done) | copy-start | bytes 3145732
Sparse Core Ops, SparseCore 0:
  36.9 48.5 all-gather.1
  91.1 186.8 all-reduce.4
  320.1 116.6 all-reduce.6
  582.5 91.4 all-reduce.8
  676.8 58.4 reduce-scatter.1
where the time goes:
time: 749 us; the launch traced here: 742 us
  waiting for transfers between devices  305 us (41%)
  blocking collectives  235 us (31%)
  other arithmetic  132 us (18%)
  matrix products  27.1 us (4%)
  local copies, waits for them, and re-layouts  24.1 us (3%)
  between operations  18.2 us (2%)
    psum x1, blocking collectives, on_device(): lax.psum(jnp.sum(normed_wide * normed_wide), ('seq', 'tensor')) / tokens_all  210 us
    psum x3, waiting for transfers between devices, broadcast(): return lax.psum(kept, axis)  208 us
    another operation x14, other arithmetic, on_device(): factor = jnp.linalg.cholesky(diag_block)  78.6 us
    all_gather x1, waiting for transfers between devices, on_device(): columns = lax.all_gather(normed, 'seq', axis=0, tiled=True)  48.6 us
    reduce_scatter x1, waiting for transfers between devices, on_device(): lax.psum_scatter(partial_value, 'seq', scatter_dimension=1, tiled=True)  48.4 us
    another operation x3, other arithmetic, on_device(): lax.linalg.triangular_solve(factor, panel_rows, left_side=False, lower=Tr...  39.4 us
    psum x1, blocking collectives, on_device(): squares = lax.psum(jnp.sum(token_values * token_values, axis=1), 'tensor')  25.6 us
  transfers between devices with their start and end apart: 5, of which 4 were waited for; matrix products, arithmetic and copies ran while one was open for 1% of the time, Pallas kernels for 0%

commit v1 on v0

--- a/solution.py
+++ b/solution.py
@@ -24,7 +24,10 @@
     blocks = column_width // row_width
     seq_index = lax.axis_index("seq")
     tensor_index = lax.axis_index("tensor")
-    columns = lax.all_gather(normed, "seq", axis=0, tiled=True)
+    size = lax.axis_size("seq")
+    shards = jnp.stack([normed for _ in range(size)])
+    shards = lax.all_to_all(shards, "seq", split_axis=0, concat_axis=0)
+    columns = jnp.concatenate(shards, axis=0)
     local_rows = lax.dynamic_slice_in_dim(columns, seq_index % blocks * row_width, row_width, 1)
     row_part = broadcast(local_rows, "tensor", seq_index // blocks)
     tokens_all = columns.shape[0]

time: 749 us -> 781 us (1.043)
  waiting for transfers between devices: 305 us -> 355 us
  blocking collectives: 235 us -> 209 us
    all_to_all x0 -> x1, waiting for transfers between devices: none -> 95.2 us  [on_device(): shards = lax.all_to_all(shards, 'seq', split_axis=0, concat_axis=0)]
    all_gather x1 -> x0, waiting for transfers between devices: 48.6 us -> none  [on_device(): columns = lax.all_gather(normed, 'seq', axis=0, tiled=True)]
    psum x1, blocking collectives: 210 us -> 183 us  [on_device(): lax.psum(jnp.sum(normed_wide * normed_wide), ('seq', 'tensor')) / tokens_all]
where the time goes in v1:
time: 781 us; the launch traced here: 774 us
  waiting for transfers between devices  355 us (45%)
  blocking collectives  209 us (27%)
  other arithmetic  130 us (17%)
  matrix products  28.8 us (4%)
  local copies, waits for them, and re-layouts  27.6 us (4%)
  between operations  18.2 us (2%)
    psum x3, waiting for transfers between devices, broadcast(): return lax.psum(kept, axis)  212 us
    psum x1, blocking collectives, on_device(): lax.psum(jnp.sum(normed_wide * normed_wide), ('seq', 'tensor')) / tokens_all  183 us
    all_to_all x1, waiting for transfers between devices, on_device(): shards = lax.all_to_all(shards, 'seq', split_axis=0, concat_axis=0)  95.2 us
    another operation x14, other arithmetic, on_device(): factor = jnp.linalg.cholesky(diag_block)  78.6 us
    reduce_scatter x1, waiting for transfers between devices, on_device(): lax.psum_scatter(partial_value, 'seq', scatter_dimension=1, tiled=True)  48.4 us
    another operation x3, other arithmetic, on_device(): lax.linalg.triangular_solve(factor, panel_rows, left_side=False, lower=Tr...  39.4 us
    psum x1, blocking collectives, on_device(): squares = lax.psum(jnp.sum(token_values * token_values, axis=1), 'tensor')  25.6 us
  transfers between devices with their start and end apart: 5, of which 4 were waited for; matrix products, arithmetic and copies ran while one was open for 1% of the time, Pallas kernels for 0%

profile of v1, /device:TPU:0, one launch (start us, length us, event | category | flops | bytes accessed | tf_op | source)
XLA Modules:
  0.0 773.8 jit_solution(15622555472383051919)
XLA Ops:
  7.2 1.3 fusion.9
  8.5 25.6 %psum.35 = f32[128]{0:T(128)S(1)} all-reduce(f32[128]{0:T(128)S(1)} %fusion.9), channel_id=1, replica_groups=mesh['seq'=16,'tensor'=8] {'tensor'}, use_global_device_ids=true, to_apply=%region_1.0 | all-reduce | flops 128 | bytes 1024 | tf_op jit(solution)/shard_map/psum | solution.py:19
  34.1 2.1 multiply_reduce_fusion
  36.2 4.5 stack.2
  40.7 4.7 all-to-all-start
  45.5 95.2 %all-to-all-done = bf16[16,128,2048]{2,1,0:T(8,128)(2,1)} async-done(((bf16[16,128,2048]{2,1,0:T(8,128)(2,1)}), bf16[16,128,2048]{2,1,0:T(8,128)(2,1)}, u32[]{:S(2)}, u32[]{:S(2)}) %all-to-all-start) | async-done | bytes 8388640 | tf_op jit(solution)/shard_map/all_to_all | solution.py:29
  140.7 5.4 dynamic-slice_select_fusion
  146.2 182.9 %psum.37 = f32[]{:T(128)} all-reduce(f32[]{:T(128)} %get-tuple-element.26), channel_id=1, replica_groups=mesh['seq'=16,'tensor'=8] {'seq','tensor'}, use_global_device_ids=true, to_apply=%region_4.5 | all-reduce | flops 1 | bytes 8 | tf_op jit(solution)/shard_map/psum | solution.py:41
  330.5 13.0 %select_add_fusion = f32[1024,2048]{0,1:T(8,128)S(1)} fusion(bf16[2048,1024]{1,0:T(8,128)(2,1)} %all-reduce.5.cloned.1.call-done, bf16[2048,2048]{1,0:T(8,128)(2,1)} %bitcast, f32[]{:T(128)S(6)} %div.53, s32[1024]{0:T(1024)S(1)} %iota_add_fusion.1, s32[2048]{0:T(1024)S(1)} %iota_add_fusion), kind=kOutput, calls=%fused_computation.2 | convolution fusion | flops 8598323200 | bytes 20983812 | tf_op jit(solution)/shard_map/dot_general | solution.py:35
  343.6 3.2 copy-done.1
  346.8 1.3 dynamic-slice_select_fusion.1
  348.2 0.5 all-reduce.9.cloned.1.call-start
  348.7 119.1 %all-reduce.7.cloned.1.call-done = f32[512,512]{0,1:T(8,128)} async-done(((f32[512,512]{0,1:T(8,128)}), f32[512,512]{0,1:T(8,128)}) %all-reduce.7.cloned.1.call-update) | async-done | bytes 1048592 | tf_op jit(solution)/shard_map/psum | solution.py:14
  467.8 0.1 convert_select_fusion
  467.9 0.3 copy.8
  468.2 0.2 fusion.15
  468.5 11.7 %cholesky.103 = f32[128,128]{1,0:T(8,128)S(1)} custom-call(f32[128,128]{1,0:T(8,128)S(1)} %cholesky.263), custom_call_target="Cholesky" | custom-call | tf_op jit(solution)/shard_map/jit(cholesky)/cholesky | solution.py:61
  480.3 9.8 %custom-call.30 = f32[1,128,128]{1,2,0:T(8,128)S(1)} custom-call(f32[1,128,128]{2,1,0:T(8,128)S(1)} %get-tuple-element.35), custom_call_target="InvertDiagBlocksLowerTriangular" | custom-call | tf_op jit(solution)/shard_map/jit(cholesky)/cholesky | solution.py:61
  490.1 0.3 fusion.21
  490.4 0.3 convolution_subtract_fusion.2
  490.8 11.7 %cholesky.215 = f32[128,128]{1,0:T(8,128)S(1)} custom-call(f32[128,128]{1,0:T(8,128)S(1)} %cholesky.267), custom_call_target="Cholesky" | custom-call | tf_op jit(solution)/shard_map/jit(cholesky)/cholesky | solution.py:61
  502.5 0.1 copy.11
  502.6 0.1 copy.10
  502.7 0.1 copy.9
  502.8 9.9 %custom-call.31 = f32[1,128,128]{1,2,0:T(8,128)S(1)} custom-call(f32[1,128,128]{2,1,0:T(8,128)S(1)} %get-tuple-element.33), custom_call_target="InvertDiagBlocksLowerTriangular" | custom-call | tf_op jit(solution)/shard_map/jit(cholesky)/cholesky | solution.py:61
  512.8 0.1 cholesky.222
  513.0 0.3 convolution_dynamic-update-slice_fusion
  513.3 1.5 convolution_subtract_fusion.3
  514.8 11.7 %cholesky.236 = f32[128,128]{1,0:T(8,128)S(1)} custom-call(f32[128,128]{1,0:T(8,128)S(1)} %cholesky.272), custom_call_target="Cholesky" | custom-call | tf_op jit(solution)/shard_map/jit(cholesky)/cholesky | solution.py:61
  526.6 0.1 copy.13
  526.7 9.8 %custom-call.32 = f32[1,128,128]{1,2,0:T(8,128)S(1)} custom-call(f32[1,128,128]{2,1,0:T(8,128)S(1)} %get-tuple-element.31), custom_call_target="InvertDiagBlocksLowerTriangular" | custom-call | tf_op jit(solution)/shard_map/jit(cholesky)/cholesky | solution.py:61
  536.5 0.3 convolution_dynamic-update-slice_fusion.1
  536.8 1.3 convolution_subtract_fusion.4
  538.1 11.9 %cholesky.253 = f32[128,128]{1,0:T(8,128)S(1)} custom-call(f32[128,128]{1,0:T(8,128)S(1)} %convolution_subtract_fusion.4), custom_call_target="Cholesky" | custom-call | tf_op jit(solution)/shard_map/jit(cholesky)/cholesky | solution.py:61
  550.1 0.1 copy.15
  550.2 0.6 compare_reduce_fusion.1
  550.8 0.6 compare_reduce_fusion
  551.4 0.6 compare_reduce_fusion.2
  554.6 0.1 select_select_fusion
  554.7 8.5 %while.1 = (s32[]{:T(128)}, f32[512,512]{0,1:T(8,128)S(1)}, s32[4,2]{0,1:T(2,128)S(1)}, f32[4,128,128]{2,1,0:T(8,128)S(1)}, s32[]{:T(128)}) while((s32[]{:T(128)}, f32[512,512]{0,1:T(8,128)S(1)}, s32[4,2]{0,1:T(2,128)S(1)}, f32[4,128,128]{2,1,0:T(8,128)S(1)}, s32[]{:T(128)}) %tuple.33), condition=%wide.while_cond, body=%wide.while_body.sunk | while | flops 2 | bytes 393321 | solution.py:62
  554.8 0.5 fusion.52
  555.3 1.4 dynamic-slice.18
  556.9 0.5 fusion.52
  557.4 1.4 dynamic-slice.18
  558.8 0.1 copy.24
  559.0 0.5 fusion.52
  559.6 1.4 dynamic-slice.18
  560.9 0.1 copy.24
  561.1 0.5 fusion.52
  561.7 1.4 dynamic-slice.18
  563.2 39.3 %custom-call.33 = f32[4,128,128]{1,2,0:T(8,128)S(1)} custom-call(f32[4,128,128]{2,1,0:T(8,128)S(1)} %get-tuple-element.10), custom_call_target="InvertDiagBlocksLowerTriangular" | custom-call | tf_op jit(solution)/shard_map/triangular_solve | solution.py:62
  602.5 1.7 fusion.41
  604.2 1.7 convolution_subtract_fusion.1
  605.8 0.6 fusion.40
  606.5 1.8 convolution_subtract_fusion
  608.3 0.6 fusion.39
  608.9 2.2 fusion.6
  611.1 0.6 convolution_convert_fusion
  611.7 1.2 maximum_select_fusion
  613.0 92.6 %all-reduce.9.cloned.1.call-done = bf16[1024,512]{0,1:T(8,128)(2,1)} async-done(((bf16[1024,512]{0,1:T(8,128)(2,1)}), bf16[1024,512]{0,1:T(8,128)(2,1)}) %all-reduce.9.cloned.1.call-update) | async-done | bytes 1048592 | tf_op jit(solution)/shard_map/psum | solution.py:14
  705.6 2.5 convolution_bitcast_fusion
  708.1 9.2 %copy.17 = f32[1024,2048]{1,0:T(8,128)} copy(f32[1024,2048]{0,1:T(8,128)} %copy-done.1) | data formatting | bytes 16777216
  717.3 1.3 copy.18
  718.6 48.4 %reduce-scatter.2.cloned.1.call-done = f32[256,32]{0,1:T(8,128)} async-done(((f32[256,512]{0,1:T(8,128)}), f32[256,32]{0,1:T(8,128)}) %reduce-scatter.2.cloned.1.call-update) | async-done | bytes 32784 | tf_op jit(solution)/shard_map/reduce_scatter | solution.py:68
  (42 shorter events, 1.0 us)
Async XLA Ops:
  7.2 698.4 %copy-start = (bf16[256,1024]{1,0:T(8,128)(2,1)S(1)}, bf16[256,1024]{1,0:T(8,128)(2,1)}, u32[]{:S(2)}) copy-start(bf16[256,1024]{1,0:T(8,128)(2,1)} %param.6) | copy-start | bytes 1572868
  40.7 100.1 %all-to-all-start = ((bf16[16,128,2048]{2,1,0:T(8,128)(2,1)}), bf16[16,128,2048]{2,1,0:T(8,128)(2,1)}, u32[]{:S(2)}, u32[]{:S(2)}) async-start(bf16[16,128,2048]{2,1,0:T(8,128)(2,1)} %stack.2), calls=%async_computation | async-start | bytes 16777216 | tf_op jit(solution)/shard_map/all_to_all | solution.py:29
  45.4 285.1 %all-reduce.5.cloned.1.call-start = ((), (), s32[]{:S(2)}) async-start(), calls=%async_computation.2 | async-start | bytes 8388608 | tf_op jit(solution)/shard_map/psum | solution.py:14
  146.2 321.6 %all-reduce.7.cloned.1.call-start = ((), (), s32[]{:S(2)}) async-start(), calls=%async_computation.3 | async-start | bytes 2097152 | tf_op jit(solution)/shard_map/psum | solution.py:14
  343.6 3.2 copy-start.1
  348.2 357.4 %all-reduce.9.cloned.1.call-start = ((), (), s32[]{:S(2)}) async-start(), calls=%async_computation.4 | async-start | bytes 2097152 | tf_op jit(solution)/shard_map/psum | solution.py:14
  468.5 34.4 %copy-start.3 = (f32[512,512]{1,0:T(8,128)}, f32[512,512]{1,0:T(8,128)S(1)}, u32[]{:S(2)}) copy-start(f32[512,512]{1,0:T(8,128)S(1)} %fusion.15) | copy-start | bytes 3145732
  613.0 154.0 %reduce-scatter.2.cloned.1.call-start = ((), (), s32[]{:S(2)}) async-start(), calls=%async_computation.5 | async-start | bytes 557056 | tf_op jit(solution)/shard_map/reduce_scatter | solution.py:68
  708.1 9.2 %copy-start.2 = (bf16[1024,512]{0,1:T(8,128)(2,1)S(1)}, bf16[1024,512]{0,1:T(8,128)(2,1)}, u32[]{:S(2)}) copy-start(bf16[1024,512]{0,1:T(8,128)(2,1)} %all-reduce.9.cloned.1.call-done) | copy-start | bytes 3145732
Sparse Core Ops, SparseCore 0:
  146.3 181.6 all-reduce.4
  348.3 119.4 all-reduce.6
  613.1 92.4 all-reduce.8
  708.5 58.4 reduce-scatter.1
